TPU v7x, 256 devices: a whole 4x4x8 slice. The times are simulated.
256 devices in a mesh: chan: 64 (over x_lo, y, z), tm: 4 (over x_hi, core).
Axes of the slice: x: 4 (x_hi: 2, x_lo: 2; x = x_hi * 2 + x_lo), y: 4, z: 8, core: 2. Of those that a mesh axis runs over, the one named last changes fastest.
Arguments:
- samples: bfloat16 [1024, 2, 16, 16384], P('chan', None, 'tm'), may hold values from -6 to 6
- filter_taps: float32 [4, 16384], replicated, may hold values from -3 to 3
Outputs:
- visibility: float32 [64, 1024, 2048], P('chan', 'tm')
All inputs are finite; a program needn't handle non-finite values.
Results may differ from a plain program's by a relative error of at most 0.01.
Values may be sent and summed in bfloat16 or wider, within the bound.
A program may use at most 128 MiB of HBM per device.

v0:
```python
import math

import jax
import jax.numpy as jnp
from jax import lax
from jax.sharding import PartitionSpec as P

ROOT = 128
TAPS = 4


def from_behind(shard, axis, by):
    count = lax.axis_size(axis)
    pairs = [(i, i + by) for i in range(count) if 0 <= i + by < count]
    return lax.ppermute(shard, axis, pairs)


def dft_tables(length):
    indices = jnp.arange(length, dtype=jnp.int32)
    product = indices[:, None] * indices[None, :] % length
    angles = product.astype(jnp.float32) * (2.0 * math.pi / length)
    cosine = jnp.cos(angles)
    sines_table = jnp.sin(angles)
    upper = jnp.stack([cosine, sines_table], axis=1)
    lower = jnp.stack([-sines_table, cosine], axis=1)
    return jnp.stack([upper, lower], axis=0).astype(jnp.bfloat16)


def channelize(window, filter_taps, number):
    filtered = filter_taps[0][None, None, None, :] * window[:, :, 0:number].astype(jnp.float32)
    for tap_index in range(1, TAPS):
        filtered = filtered + filter_taps[tap_index][None, None, None, :] * window[
            :, :, tap_index : tap_index + number
        ].astype(jnp.float32)
    filtered = filtered.astype(jnp.bfloat16).reshape(window.shape[0], 2, number, ROOT, ROOT)
    matrix = dft_tables(ROOT)
    first_pass = jnp.einsum(
        "pcra,irsab->ipscb", matrix, filtered, preferred_element_type=jnp.float32
    )
    indices = jnp.arange(ROOT, dtype=jnp.int32)
    product = indices[:, None] * indices[None, :] % (ROOT * ROOT)
    angles = product.astype(jnp.float32) * (2.0 * math.pi / (ROOT * ROOT))
    cosine = jnp.cos(angles)
    sines_table = jnp.sin(angles)
    real_part = first_pass[:, 0]
    imag_part = first_pass[:, 1]
    twisted = jnp.stack(
        [
            (real_part * cosine + imag_part * sines_table) / ROOT,
            (imag_part * cosine - real_part * sines_table) / ROOT,
        ],
        axis=1,
    ).astype(jnp.bfloat16)
    spectra = jnp.einsum("pdqb,iqscb->ipsdc", matrix, twisted, preferred_element_type=jnp.float32)
    return spectra.astype(jnp.bfloat16)


def hermitian_operands(member):
    flattened = member.reshape(member.shape[0], -1)
    swapped = jnp.concatenate([-member[:, 1:2], member[:, 0:1]], axis=1).reshape(
        member.shape[0], -1
    )
    return (flattened, jnp.concatenate([flattened, swapped], axis=0))


def correlate(row_side, col_side, factor):
    product = lax.dot_general(
        row_side, col_side, (((1,), (1,)), ((), ())), preferred_element_type=jnp.float32
    )
    return product * factor


def body(samples, filter_taps):
    number = samples.shape[2]
    history = from_behind(samples[:, :, number - (TAPS - 1) :, :], "tm", 1)
    frames = jnp.concatenate([history, samples], axis=2)
    spectra = lax.all_to_all(
        channelize(frames, filter_taps, number), "chan", split_axis=3, concat_axis=0, tiled=True
    )
    factor = 1.0 / (number * lax.axis_size("tm") * spectra.shape[3] * spectra.shape[4])
    flattened, col_side = hermitian_operands(spectra)
    visibility = lax.psum_scatter(
        correlate(flattened, col_side, factor).astype(jnp.bfloat16),
        "tm",
        scatter_dimension=0,
        tiled=True,
    ).astype(jnp.float32)
    return visibility[None]


def solution(mesh):
    placed = (P("chan", None, "tm", None), P())
    return jax.shard_map(
        body, mesh=mesh, in_specs=placed, out_specs=P("chan", "tm", None), check_vma=False
    )
```

profile of v0, /device:TPU:1, one launch (start us, length us, event | category | flops | bytes accessed | tf_op | source)
XLA Modules:
  0.0 289.8 jit_solution(10963608220992393547)
XLA Ops:
  6.5 4.7 %slice.37 = bf16[16,2,3,16384]{3,2,1,0:T(4,128)(2,1)S(1)} slice(bf16[16,2,4,16384]{3,2,1,0:T(4,128)(2,1)} %param.2), slice={[0:16], [0:2], [1:4], [0:16384]} | slice | bytes 6291456 | tf_op jit(solution)/shard_map/slice | solution.py:75
  11.3 2.3 copy.29
  13.6 6.5 %collective-permute-start = (bf16[16,2,3,16384]{3,0,2,1:T(8,128)(2,1)S(1)}, bf16[16,2,3,16384]{3,0,2,1:T(8,128)(2,1)S(1)}, u32[]{:S(2)}, u32[]{:S(2)}) collective-permute-start(bf16[16,2,3,16384]{3,0,2,1:T(8,128)(2,1)S(1)} %copy.29), channel_id=1, source_target_pairs={{0,1},{1,2},{2,3},{4,5},{5,6},{6,7},{8,9},{9,10},{10,11},{12,13},{... | collective-permute-start | bytes 9437192 | tf_op jit(solution)/shard_map/ppermute | solution.py:15
  20.3 0.3 negate_convert_fusion
  21.1 33.0 %collective-permute-done = bf16[16,2,3,16384]{3,0,2,1:T(8,128)(2,1)S(1)} collective-permute-done((bf16[16,2,3,16384]{3,0,2,1:T(8,128)(2,1)S(1)}, bf16[16,2,3,16384]{3,0,2,1:T(8,128)(2,1)S(1)}, u32[]{:S(2)}, u32[]{:S(2)}) %collective-permute-start) | collective-permute-done | bytes 3145760 | tf_op jit(solution)/shard_map/ppermute | solution.py:15
  54.1 2.7 copy.12
  56.8 14.5 %add_convert_fusion = bf16[16,2,4,16384]{3,2,1,0:T(4,128)(2,1)} fusion(bf16[16,2,4,16384]{3,2,1,0:T(4,128)(2,1)S(1)} %copy-done, bf16[16,2,3,16384]{3,2,1,0:T(4,128)(2,1)S(1)} %copy.12, f32[16384]{0:T(1024)S(1)} %bitcast.50, f32[16384]{0:T(1024)S(1)} %bitcast.51, f32[16384]{0:T(1024)S(1)} %bitcast.49, f32[16384]{0:T(1024)S(1)} %bitcast.48), kind=kLoop, calls=%fused_computation.10 | loop fusion | flops 44040192 | bytes 11796480 | tf_op jit(solution)/shard_map/convert_element_type | solution.py:35
  71.3 8.5 %reshape.125 = bf16[16,2,4,128,128]{4,3,2,1,0:T(8,128)(2,1)} reshape(bf16[16,2,4,16384]{3,2,1,0:T(4,128)(2,1)} %add_convert_fusion) | data formatting | bytes 8388608 | tf_op jit(solution)/shard_map/reshape | solution.py:35
  79.8 3.5 %fusion.14 = f32[16,2,4,128,128]{3,4,1,2,0:T(8,128)S(1)} fusion(bf16[1,128,2,128]{3,1,2,0:T(8,128)(2,1)S(1)} %get-tuple-element.14, bf16[1,128,2,128]{3,1,2,0:T(8,128)(2,1)S(1)} %get-tuple-element.13, bf16[16,2,4,128,128]{4,3,2,1,0:T(8,128)(2,1)} %reshape.125), kind=kOutput, calls=%fused_computation.24 | convolution fusion | flops 1074003968 | bytes 12713984 | tf_op jit(solution)/shard_map/pcra,irsab->ipscb/dot_general | solution.py:37
  83.3 1.5 multiply_convert_fusion.2
  84.8 3.3 %fusion.6 = bf16[16,2,4,128,128]{3,4,1,2,0:T(8,128)(2,1)} fusion(bf16[16,1,4,128,128]{3,4,1,2,0:T(8,128)(2,1)S(1)} %get-tuple-element.6, bf16[16,1,4,128,128]{3,4,1,2,0:T(8,128)(2,1)S(1)} %get-tuple-element.5, bf16[1,128,2,128]{3,1,2,0:T(8,128)(2,1)S(1)} %get-tuple-element.14, bf16[1,128,2,128]{3,1,2,0:T(8,128)(2,1)S(1)} %get-tuple-element.13), kind=kOutput, calls=%fused_computation.11 | convolution fusion | flops 1084489728 | bytes 8519680 | tf_op jit(solution)/shard_map/pdqb,iqscb->ipsdc/dot_general | solution.py:54
  88.0 11.3 %copy.15 = bf16[16,2,4,128,128]{4,1,2,0,3:T(2,128)(2,1)} copy(bf16[16,2,4,128,128]{3,4,1,2,0:T(8,128)(2,1)} %fusion.6) | data formatting | bytes 8388608 | tf_op jit(solution)/shard_map/convert_element_type | solution.py:55
  99.3 78.0 %all_to_all.18 = bf16[16,2,4,128,128]{4,1,2,0,3:T(2,128)(2,1)S(1)} all-to-all(bf16[16,2,4,128,128]{4,1,2,0,3:T(2,128)(2,1)} %copy.15), channel_id=1, replica_groups=mesh['chan'=64,'tm'=4] {'chan'}, dimensions={3} | all-to-all | bytes 8388608 | tf_op jit(solution)/shard_map/all_to_all | solution.py:77
  177.3 0.5 copy.16
  177.9 2.9 copy.18
  180.8 6.7 %copy.17 = bf16[64,16,2,4,2,128]{5,4,3,2,1,0:T(2,128)(2,1)} copy(bf16[64,16,2,4,2,128]{5,1,4,0,3,2:T(8,128)(2,1)S(1)} %bitcast.46) | data formatting | bytes 8388608 | tf_op jit(solution)/shard_map/all_to_all | solution.py:77
  187.5 7.8 %reshape.126 = bf16[1024,2048]{1,0:T(8,128)(2,1)} reshape(bf16[64,16,2,4,2,128]{5,4,3,2,1,0:T(2,128)(2,1)} %copy.17) | data formatting | bytes 8388608 | tf_op jit(solution)/shard_map/reshape | solution.py:59
  195.3 2.6 slice_negate_fusion
  197.9 0.4 pad_maximum_fusion.1
  198.3 6.3 %copy.19 = bf16[1024,2,4,2,128]{4,3,2,1,0:T(2,128)(2,1)} copy(bf16[1024,2,4,2,128]{4,0,3,2,1:T(8,128)(2,1)S(1)} %pad_maximum_fusion.1) | data formatting | bytes 8388608 | tf_op jit(solution)/shard_map/concatenate | solution.py:60
  204.6 7.8 %reshape.127 = bf16[1024,2048]{1,0:T(8,128)(2,1)} reshape(bf16[1024,2,4,2,128]{4,3,2,1,0:T(2,128)(2,1)} %copy.19) | data formatting | bytes 8388608 | tf_op jit(solution)/shard_map/reshape | solution.py:60
  212.4 14.8 %multiply_convert_fusion = bf16[1024,2048]{1,0:T(8,128)(2,1)} fusion(bf16[1024,2048]{1,0:T(8,128)(2,1)} %reshape.126, bf16[1024,2048]{1,0:T(8,128)(2,1)} %reshape.127), kind=kOutput, calls=%fused_computation.9 | convolution fusion | flops 8610906112 | bytes 12582912 | tf_op jit(solution)/shard_map/dot_general | solution.py:67
  227.3 52.9 %reduce-scatter.2.cloned.1.call-done = bf16[256,2048]{1,0:T(8,128)(2,1)} async-done(((bf16[1024,2048]{1,0:T(8,128)(2,1)}), bf16[256,2048]{1,0:T(8,128)(2,1)}) %reduce-scatter.2.cloned.1.call-update) | async-done | bytes 1048592 | tf_op jit(solution)/shard_map/reduce_scatter | solution.py:82
  280.1 2.8 bitcast_convert_fusion.1
  (10 shorter events, 0.8 us)
Async XLA Ops:
  6.5 273.6 %reduce-scatter.2.cloned.1.call-start = ((), (), s32[]{:S(2)}) async-start(), calls=%async_computation.2 | async-start | bytes 5242880 | tf_op jit(solution)/shard_map/reduce_scatter | solution.py:82
  11.2 9.7 %copy-start.1 = (f32[4,16384]{1,0:T(4,128)S(1)}, f32[4,16384]{1,0:T(4,128)}, u32[]{:S(2)}) copy-start(f32[4,16384]{1,0:T(4,128)} %param.3) | copy-start | bytes 786436
  13.5 43.2 %copy-start = (bf16[16,2,4,16384]{3,2,1,0:T(4,128)(2,1)S(1)}, bf16[16,2,4,16384]{3,2,1,0:T(4,128)(2,1)}, u32[]{:S(2)}) copy-start(bf16[16,2,4,16384]{3,2,1,0:T(4,128)(2,1)} %param.2) | copy-start | bytes 12582916
  13.6 40.5 %collective-permute-start = (bf16[16,2,3,16384]{3,0,2,1:T(8,128)(2,1)S(1)}, bf16[16,2,3,16384]{3,0,2,1:T(8,128)(2,1)S(1)}, u32[]{:S(2)}, u32[]{:S(2)}) collective-permute-start(bf16[16,2,3,16384]{3,0,2,1:T(8,128)(2,1)S(1)} %copy.29), channel_id=1, source_target_pairs={{0,1},{1,2},{2,3},{4,5},{5,6},{6,7},{8,9},{9,10},{10,11},{12,13},{... | collective-permute-start | bytes 9437192 | tf_op jit(solution)/shard_map/ppermute | solution.py:15
Sparse Core Ops, SparseCore 0:
  227.4 52.6 reduce-scatter.1
where the time goes:
time: 291 us; the launch traced here: 290 us
  waiting for transfers between devices  85.8 us (29%)
  blocking collectives  78 us (27%)
  local copies, waits for them, and re-layouts  61.7 us (21%)
  other arithmetic  22.6 us (8%)
  matrix products  21.6 us (7%)
  between operations  13.5 us (5%)
  starting transfers between devices  6.49 us (2%)
    all_to_all x1, blocking collectives, body(): lax.all_to_all(channelize(frames, filter_taps, number), 'chan', split_axi...  78 us
    reduce_scatter x1, waiting for transfers between devices, body(): lax.psum_scatter(correlate(flattened, col_side, factor).astype(jnp.bfloat...  52.9 us
    ppermute x1, waiting for transfers between devices, from_behind(): return lax.ppermute(shard, axis, pairs)  33 us
    dot_general x1, matrix products, correlate(): lax.dot_general(row_side, col_side, (((1,), (1,)), ((), ())), preferred_e...  14.8 us
    convert_element_type x1, other arithmetic, channelize(): filtered.astype(jnp.bfloat16)  14.5 us
    convert_element_type x1, local copies, waits for them, and re-layouts, channelize(): return spectra.astype(jnp.bfloat16)  11.3 us
    all_to_all x3, local copies, waits for them, and re-layouts, body(): lax.all_to_all(channelize(frames, filter_taps, number), 'chan', split_axi...  10.1 us
    reshape x1, local copies, waits for them, and re-layouts, channelize(): filtered.astype(jnp.bfloat16)  8.48 us
  transfers between devices with their start and end apart: 2, of which 2 were waited for; matrix products, arithmetic and copies ran while one was open for 0% of the time, Pallas kernels for 0%

commit v1 on v0

v1 whole, which is shorter than its diff:
```python
import functools
import math

import jax
import jax.numpy as jnp
import numpy as np
from jax import lax
from jax.experimental import pallas as pl
from jax.experimental.pallas import tpu as pltpu
from jax.sharding import PartitionSpec as P

ROOT = 128
TAPS = 4
SPEC = 4
INP = 16
MESH = pl.DeviceIdType.MESH
BF = jnp.bfloat16
F32 = jnp.float32


def dft_table():
    indices = np.arange(ROOT)
    angles = (indices[:, None] * indices[None, :] % ROOT) * (2.0 * math.pi / ROOT)
    cosine, sine = np.cos(angles), np.sin(angles)
    upper = np.concatenate([cosine, sine], axis=1)
    lower = np.concatenate([-sine, cosine], axis=1)
    return np.concatenate([upper, lower], axis=0)


def twiddle_table():
    indices = np.arange(ROOT)
    angles = (indices[:, None] * indices[None, :]) * (2.0 * math.pi / (ROOT * ROOT))
    return np.stack([np.cos(angles), np.sin(angles)]) / ROOT


def place():
    chan, tm = lax.axis_index("chan"), lax.axis_index("tm")
    return chan // 32, (chan // 8) % 4, chan % 8, tm


def turn_kernel(
    x_ref, taps_ref, m_ref, tw_ref, out_ref,
    xin, wide, frames, turned, snd, mid,
    in_sem, halo_s, halo_r, z_s, z_r, xy_s, xy_r, loc_sem,
):
    x_lo, y, z, tm = place()
    xy = x_lo * 4 + y

    def chan_of(xy_, z_):
        return xy_ * 8 + z_

    def other_xy(k):
        return ((x_lo + k // 4) % 2) * 4 + (y + k % 4) % 4

    for i in range(INP):
        pltpu.make_async_copy(x_ref.at[i], xin.at[i], in_sem.at[i]).start()

    barrier = pltpu.get_barrier_semaphore()
    for k in range(1, 8):
        pl.semaphore_signal(barrier, inc=1, device_id={"chan": chan_of(xy, (z + k) % 8)}, device_id_type=MESH)
        pl.semaphore_signal(barrier, inc=1, device_id={"chan": chan_of(other_xy(k), z)}, device_id_type=MESH)

    for k in (1, 3):
        pl.semaphore_signal(barrier, inc=1, device_id={"tm": (tm + k) % 4}, device_id_type=MESH)
    pl.semaphore_wait(barrier, 16)

    @pl.when(tm == 0)
    def _():
        frames[0:3] = jnp.zeros((3, INP, 2, ROOT, ROOT), BF)

    def relayout(i, carry):
        pltpu.make_async_copy(x_ref.at[i], xin.at[i], in_sem.at[i]).wait()
        for p in range(2):
            wide[p] = xin[i, p].astype(F32)
            for s in range(SPEC):
                frames[3 + s, i, p] = wide[p, pl.ds(s, ROOT, stride=SPEC), :].astype(BF)
        return carry

    lax.fori_loop(0, INP, relayout, 0)

    def halo(j):
        return pltpu.make_async_remote_copy(
            src_ref=frames.at[4 + j], dst_ref=frames.at[j],
            send_sem=halo_s.at[j], recv_sem=halo_r.at[j],
            device_id={"tm": (tm + 1) % 4}, device_id_type=MESH,
        )

    @pl.when(tm < 3)
    def _():
        for j in (2, 1, 0):
            halo(j).start()

    def spectrum(s):
        def pair(step, carry):
            sides = []
            for j in range(2):
                i = step * 2 + j
                parts = []
                for p in range(2):
                    total = taps_ref[0] * frames[s, i, p].astype(F32)
                    for k in range(1, TAPS):
                        total = total + taps_ref[k] * frames[s + k, i, p].astype(F32)
                    parts.append(total.astype(BF))
                sides.append(jnp.concatenate(parts, axis=0))
            both = jnp.concatenate(sides, axis=1)
            first = jnp.dot(m_ref[...], both, preferred_element_type=F32)
            rows = []
            for j in range(2):
                real = first[:ROOT, j * ROOT : (j + 1) * ROOT]
                imag = first[ROOT:, j * ROOT : (j + 1) * ROOT]
                cosine, sine = tw_ref[0], tw_ref[1]
                rows.append(
                    jnp.concatenate(
                        [(real * cosine + imag * sine).astype(BF), (imag * cosine - real * sine).astype(BF)],
                        axis=1,
                    )
                )
            second = lax.dot_general(
                m_ref[...], jnp.concatenate(rows, axis=0), (((1,), (1,)), ((), ())), preferred_element_type=F32
            )
            for j in range(2):
                turned[pl.ds(step * 2 + j, 2 * ROOT, stride=INP), :] = second[:, j * ROOT : (j + 1) * ROOT]
            return carry

        lax.fori_loop(0, INP // 2, pair, 0)

        def pack(g, carry):
            for p in range(2):
                for d in range(2):
                    row = pl.multiple_of((p * ROOT + 2 * g + d) * INP, INP)
                    lane = (p * 2 + d) * ROOT
                    snd[s, g % 8, g // 8, :, lane : lane + ROOT] = turned[pl.ds(row, INP), :].astype(BF)
            return carry

        lax.fori_loop(0, 64, pack, 0)

    def z_copy(s, k):
        to = (z + k) % 8
        return pltpu.make_async_remote_copy(
            src_ref=snd.at[s, to], dst_ref=mid.at[s, z],
            send_sem=z_s.at[s, k], recv_sem=z_r.at[s, k],
            device_id={"chan": chan_of(xy, to)}, device_id_type=MESH,
        )

    def xy_copy(s, k):
        to = other_xy(k)
        return pltpu.make_async_remote_copy(
            src_ref=mid.at[s, :, to], dst_ref=out_ref.at[s, xy],
            send_sem=xy_s.at[s, k], recv_sem=xy_r.at[s, k],
            device_id={"chan": chan_of(to, z)}, device_id_type=MESH,
        )

    def z_own(s):
        return pltpu.make_async_copy(snd.at[s, z], mid.at[s, z], loc_sem.at[s, 0])

    def xy_own(s):
        return pltpu.make_async_copy(mid.at[s, :, xy], out_ref.at[s, xy], loc_sem.at[s, 1])

    def send(s):
        for k in (4, 3, 5, 2, 6, 1, 7):
            z_copy(s, k).start()
        z_own(s).start()

    def forward(s):
        for k in range(1, 8):
            z_copy(s, k).wait_recv()
        z_own(s).wait()
        for k in range(1, 8):
            xy_copy(s, k).start()
        xy_own(s).start()

    def arrive(j):
        @pl.when(tm > 0)
        def _():
            halo(j).wait_recv()

    spectrum(3)
    send(3)
    arrive(2)
    spectrum(2)
    send(2)
    arrive(1)
    spectrum(1)
    send(1)
    forward(3)
    arrive(0)
    spectrum(0)
    send(0)
    forward(2)
    forward(1)
    forward(0)
    for s in range(SPEC):
        for k in range(1, 8):
            xy_copy(s, k).wait_recv()
        xy_own(s).wait()
    for s in range(SPEC):
        for k in range(1, 8):
            z_copy(s, k).wait_send()
            xy_copy(s, k).wait_send()

    @pl.when(tm < 3)
    def _():
        for j in range(3):
            halo(j).wait_send()


def turn(samples, taps):
    x = samples.reshape(INP, 2, SPEC, ROOT, ROOT).transpose(0, 1, 3, 2, 4).reshape(INP, 2, SPEC * ROOT, ROOT)
    vmem = pl.BlockSpec(memory_space=pltpu.VMEM)
    hbm = pl.BlockSpec(memory_space=pl.ANY)
    return pl.pallas_call(
        turn_kernel,
        out_shape=jax.ShapeDtypeStruct((SPEC, 8, 8, INP, 4 * ROOT), BF),
        in_specs=[hbm, vmem, vmem, vmem],
        out_specs=hbm,
        scratch_shapes=[
            pltpu.VMEM((INP, 2, SPEC * ROOT, ROOT), BF),
            pltpu.VMEM((2, SPEC * ROOT, ROOT), F32),
            pltpu.VMEM((7, INP, 2, ROOT, ROOT), BF),
            pltpu.VMEM((2 * ROOT * INP, ROOT), F32),
            pltpu.VMEM((SPEC, 8, 8, INP, 4 * ROOT), BF),
            pltpu.VMEM((SPEC, 8, 8, INP, 4 * ROOT), BF),
            pltpu.SemaphoreType.DMA((INP,)),
            pltpu.SemaphoreType.DMA((3,)),
            pltpu.SemaphoreType.DMA((3,)),
            pltpu.SemaphoreType.DMA((SPEC, 8)),
            pltpu.SemaphoreType.DMA((SPEC, 8)),
            pltpu.SemaphoreType.DMA((SPEC, 8)),
            pltpu.SemaphoreType.DMA((SPEC, 8)),
            pltpu.SemaphoreType.DMA((SPEC, 2)),
        ],
        compiler_params=pltpu.CompilerParams(
            collective_id=0, has_side_effects=True, vmem_limit_bytes=48 * 2**20
        ),
    )(x, taps.reshape(TAPS, ROOT, ROOT), jnp.asarray(dft_table(), BF), jnp.asarray(twiddle_table(), F32))


def corr_kernel(a_ref, out_ref, sib_snd, sib_rcv, x_snd, x_rcv, sib_s, sib_r, x_s, x_r):
    tm = lax.axis_index("tm")
    x_hi, core = tm // 2, tm % 2
    sibling = x_hi * 2 + 1 - core
    partner = (1 - x_hi) * 2 + core
    factor = 1.0 / 4096.0

    barrier = pltpu.get_barrier_semaphore()
    for other in (sibling, partner):
        pl.semaphore_signal(barrier, inc=1, device_id={"tm": other}, device_id_type=MESH)
    pl.semaphore_wait(barrier, 2)

    nt = (((1,), (1,)), ((), ()))

    def block(owner, j):
        rows = pl.ds(pl.multiple_of(owner * 256, 256), 256)
        cols = pl.ds(pl.multiple_of(j * 256, 256), 256)
        real = jnp.zeros((256, 256), F32)
        imag = jnp.zeros((256, 256), F32)
        for s in range(SPEC):
            left, right = a_ref[s, rows, :], a_ref[s, cols, :]
            real = real + lax.dot_general(left, right, nt, preferred_element_type=F32)
            imag = imag + lax.dot_general(left[:, 256:], right[:, :256], nt, preferred_element_type=F32)
            imag = imag - lax.dot_general(left[:, :256], right[:, 256:], nt, preferred_element_type=F32)
        return real * factor, imag * factor

    def sib_copy(h, j):
        return pltpu.make_async_remote_copy(
            src_ref=sib_snd.at[h, j], dst_ref=sib_rcv.at[h, j], send_sem=sib_s.at[h, j], recv_sem=sib_r.at[h, j],
            device_id={"tm": sibling}, device_id_type=MESH,
        )

    def x_copy(j):
        return pltpu.make_async_remote_copy(
            src_ref=x_snd.at[j], dst_ref=x_rcv.at[j], send_sem=x_s.at[j], recv_sem=x_r.at[j],
            device_id={"tm": partner}, device_id_type=MESH,
        )

    def far(j, carry):
        real, imag = block((1 - x_hi) * 2 + 1 - core, j)
        sib_snd[0, j, 0] = real.astype(BF)
        sib_snd[0, j, 1] = imag.astype(BF)
        sib_copy(0, j).start()
        real, imag = block((1 - x_hi) * 2 + core, j)
        sib_copy(0, j).wait_recv()
        x_snd[j, 0] = (real + sib_rcv[0, j, 0].astype(F32)).astype(BF)
        x_snd[j, 1] = (imag + sib_rcv[0, j, 1].astype(F32)).astype(BF)
        x_copy(j).start()
        return carry

    lax.fori_loop(0, 4, far, 0)

    def near(j, carry):
        real, imag = block(x_hi * 2 + 1 - core, j)
        sib_snd[1, j, 0] = real.astype(BF)
        sib_snd[1, j, 1] = imag.astype(BF)
        sib_copy(1, j).start()
        real, imag = block(x_hi * 2 + core, j)
        sib_copy(1, j).wait_recv()
        out_ref[:, pl.ds(pl.multiple_of(j * 256, 256), 256)] = real + sib_rcv[1, j, 0].astype(F32)
        out_ref[:, pl.ds(pl.multiple_of(j * 256 + 1024, 256), 256)] = imag + sib_rcv[1, j, 1].astype(F32)
        return carry

    lax.fori_loop(0, 4, near, 0)

    def finish(j, carry):
        x_copy(j).wait_recv()
        out_ref[:, pl.ds(pl.multiple_of(j * 256, 256), 256)] += x_rcv[j, 0].astype(F32)
        out_ref[:, pl.ds(pl.multiple_of(j * 256 + 1024, 256), 256)] += x_rcv[j, 1].astype(F32)
        return carry

    lax.fori_loop(0, 4, finish, 0)
    for j in range(4):
        sib_copy(0, j).wait_send()
        sib_copy(1, j).wait_send()
        x_copy(j).wait_send()


def corr(spectra):
    vmem = pl.BlockSpec(memory_space=pltpu.VMEM)
    return pl.pallas_call(
        corr_kernel,
        out_shape=jax.ShapeDtypeStruct((256, 2048), F32),
        in_specs=[vmem],
        out_specs=vmem,
        scratch_shapes=[
            pltpu.VMEM((2, 4, 2, 256, 256), BF),
            pltpu.VMEM((2, 4, 2, 256, 256), BF),
            pltpu.VMEM((4, 2, 256, 256), BF),
            pltpu.VMEM((4, 2, 256, 256), BF),
            pltpu.SemaphoreType.DMA((2, 4)),
            pltpu.SemaphoreType.DMA((2, 4)),
            pltpu.SemaphoreType.DMA((4,)),
            pltpu.SemaphoreType.DMA((4,)),
        ],
        compiler_params=pltpu.CompilerParams(
            collective_id=1, has_side_effects=True, vmem_limit_bytes=48 * 2**20
        ),
    )(spectra)


def body(samples, filter_taps):
    spectra = turn(samples, filter_taps).reshape(SPEC, 1024, 4 * ROOT)
    return corr(spectra)[None]


def solution(mesh):
    placed = (P("chan", None, "tm", None), P())
    return jax.shard_map(
        body, mesh=mesh, in_specs=placed, out_specs=P("chan", "tm", None), check_vma=False
    )
```

time: 291 us -> 161 us (0.55)
  Pallas kernels: 0 us -> 155 us
  waiting for transfers between devices: 85.8 us -> 0 us
  blocking collectives: 78 us -> 0 us
  local copies, waits for them, and re-layouts: 61.7 us -> 6.02 us
  other arithmetic: 22.6 us -> 0 us
  matrix products: 21.6 us -> 0 us
  between operations: 13.5 us -> 0.04 us
  starting transfers between devices: 6.49 us -> 0 us
    pallas_call x0 -> x2, Pallas kernels: none -> 155 us  [the longest x1 123 us: turn(): pl.pallas_call(turn_kernel, out_shape=jax.ShapeDtypeStruct((SPEC, 8, 8, I...]
    all_to_all x1 -> x0, blocking collectives: 78 us -> none  [body(): lax.all_to_all(channelize(frames, filter_taps, number), 'chan', split_axi...]
    reduce_scatter x1 -> x0, waiting for transfers between devices: 52.9 us -> none  [body(): lax.psum_scatter(correlate(flattened, col_side, factor).astype(jnp.bfloat...]
    ppermute x1 -> x0, waiting for transfers between devices: 33 us -> none  [from_behind(): return lax.ppermute(shard, axis, pairs)]
    reshape x3 -> x0, local copies, waits for them, and re-layouts: 24.1 us -> none  [the longest x1 8.48 us: channelize(): filtered.astype(jnp.bfloat16)]
    dot_general x3 -> x0, matrix products: 21.6 us -> none  [the longest x1 14.8 us: correlate(): lax.dot_general(row_side, col_side, (((1,), (1,)), ((), ())), preferred_e...]
    convert_element_type x1 -> x0, other arithmetic: 14.5 us -> none  [channelize(): filtered.astype(jnp.bfloat16)]
    convert_element_type x1 -> x0, local copies, waits for them, and re-layouts: 11.3 us -> none  [channelize(): return spectra.astype(jnp.bfloat16)]
  transfers between devices with their start and end apart: 2 -> 0, of which waited for: 2 -> 0; matrix products, arithmetic and copies ran while one was open for 0% -> 0% of each run, Pallas kernels for 0% -> 0%
where the time goes in v1:
time: 161 us
  Pallas kernels  155 us (96%)
  local copies, waits for them, and re-layouts  6.02 us (4%)
    pallas_call x1, Pallas kernels, turn(): pl.pallas_call(turn_kernel, out_shape=jax.ShapeDtypeStruct((SPEC, 8, 8, I...  123 us
    pallas_call x1, Pallas kernels, corr(): pl.pallas_call(corr_kernel, out_shape=jax.ShapeDtypeStruct((256, 2048), F...  32.4 us
    unnamed x8, local copies, waits for them, and re-layouts  6.02 us

profile of v1, /device:TPU:1, one launch (start us, length us, event | category | flops | bytes accessed | tf_op | source)
XLA Modules:
  0.0 161.3 jit_solution(2770949834130964301)
XLA Ops:
  0.0 1.0 copy.8
  1.0 0.0 copy-start.1
  1.0 0.9 copy-done.1
  1.9 0.0 copy-start.2
  1.9 0.9 copy-done.2
  2.8 122.9 %shard_map.46 = bf16[4,8,8,16,512]{4,3,2,1,0:T(8,128)(2,1)S(1)} custom-call(bf16[16,2,512,128]{3,2,1,0:T(8,128)(2,1)} %bitcast.14, f32[4,128,128]{2,1,0:T(8,128)S(1)} %bitcast.13, bf16[256,256]{1,0:T(8,128)(2,1)S(1)} %copy-done.2, f32[2,128,128]{2,1,0:T(8,128)S(1)} %copy-done.1), custom_call_target="tpu_custom_call" | custom-call | tf_op jit(solution)/shard_map/pallas_call | solution.py:211
  125.7 0.0 copy-start
  125.7 1.9 %copy-done = bf16[4,8,8,16,512]{4,3,2,1,0:T(8,128)(2,1)} copy-done((bf16[4,8,8,16,512]{4,3,2,1,0:T(8,128)(2,1)}, bf16[4,8,8,16,512]{4,3,2,1,0:T(8,128)(2,1)S(1)}, u32[]{:S(2)}) %copy-start) | copy-done | bytes 4194328
  127.6 32.4 %shard_map.47 = f32[256,2048]{1,0:T(8,128)S(1)} custom-call(bf16[4,1024,512]{2,1,0:T(8,128)(2,1)} %bitcast.11), custom_call_target="tpu_custom_call" | custom-call | tf_op jit(solution)/shard_map/pallas_call | solution.py:318
  160.0 1.3 copy.10
Async XLA Ops:
  1.0 0.9 copy-start.1
  1.9 0.9 copy-start.2
  125.7 1.9 %copy-start = (bf16[4,8,8,16,512]{4,3,2,1,0:T(8,128)(2,1)}, bf16[4,8,8,16,512]{4,3,2,1,0:T(8,128)(2,1)S(1)}, u32[]{:S(2)}) copy-start(bf16[4,8,8,16,512]{4,3,2,1,0:T(8,128)(2,1)S(1)} %shard_map.46) | copy-start | bytes 12582916

commit v2 on v1

v2 whole, which is shorter than its diff:
```python
import math

import jax
import jax.numpy as jnp
import numpy as np
from jax import lax
from jax.experimental import pallas as pl
from jax.experimental.pallas import tpu as pltpu
from jax.sharding import PartitionSpec as P

ROOT = 128
TAPS = 4
SPEC = 4
INP = 16
WIDE = 4 * ROOT
LATE = 7
Z_FIRST = (3, 2, 1)
MESH = pl.DeviceIdType.MESH
BF = jnp.bfloat16
F32 = jnp.float32
NT = (((1,), (1,)), ((), ()))


def dft_table():
    indices = np.arange(ROOT)
    angles = (indices[:, None] * indices[None, :] % ROOT) * (2.0 * math.pi / ROOT)
    cosine, sine = np.cos(angles), np.sin(angles)
    upper = np.concatenate([cosine, sine], axis=1)
    lower = np.concatenate([-sine, cosine], axis=1)
    return np.concatenate([upper, lower], axis=0)


def twiddle_table():
    indices = np.arange(ROOT)
    angles = (indices[:, None] * indices[None, :]) * (2.0 * math.pi / (ROOT * ROOT))
    return np.stack([np.cos(angles), np.sin(angles)]) / ROOT


def tables():
    quarters = dft_table().reshape(2, ROOT, 2, ROOT).transpose(0, 2, 1, 3).reshape(4, ROOT, ROOT)
    return np.concatenate([twiddle_table(), quarters]).astype(np.float32)


def kernel(
    x_ref, taps_ref, tab_ref, out_ref,
    xin, tin, taps, m, tw, wide, frames, turned, snd, mid, rcv, late,
    acc, mine, sib_snd, sib_rcv, x_snd, x_rcv,
    d1, d2, d1_snd, d1_rcv, d2_snd, d2_rcv, d1_xs, d1_xr, d2_xs, d2_xr,
    in_sem, const_sem, halo_s, halo_r, z_s, z_r, xy_s, xy_r, xl_s, xl_r, loc_sem,
    sib_s, sib_r, x_s, x_r, ds_s, ds_r, dx_s, dx_r,
):
    chan, tm = lax.axis_index("chan"), lax.axis_index("tm")
    x_lo, y, z = chan // 32, (chan // 8) % 4, chan % 8
    x_hi, core = tm // 2, tm % 2
    xy = x_lo * 4 + y
    sibling = x_hi * 2 + 1 - core
    partner = (1 - x_hi) * 2 + core

    def chan_of(xy_, z_):
        return xy_ * 8 + z_

    def other_xy(k):
        return ((x_lo + k // 4) % 2) * 4 + (y + k % 4) % 4

    constants = [
        pltpu.make_async_copy(taps_ref, tin, const_sem.at[0]),
        pltpu.make_async_copy(tab_ref, tw, const_sem.at[1]),
    ]
    for i in range(INP):
        pltpu.make_async_copy(x_ref.at[i], xin.at[i], in_sem.at[i]).start()
    for copy in constants:
        copy.start()

    barrier = pltpu.get_barrier_semaphore()
    for k in range(1, 8):
        pl.semaphore_signal(barrier, inc=1, device_id={"chan": chan_of(xy, (z + k) % 8)}, device_id_type=MESH)
        pl.semaphore_signal(barrier, inc=1, device_id={"chan": chan_of(other_xy(k), z)}, device_id_type=MESH)
    for k in range(1, 4):
        pl.semaphore_signal(barrier, inc=1, device_id={"tm": (tm + k) % 4}, device_id_type=MESH)

    @pl.when(tm == 0)
    def _():
        frames[0:3] = jnp.zeros((3, INP, 2, ROOT, ROOT), BF)

    for copy in constants:
        copy.wait()
    for k in range(TAPS):
        taps[k] = tin[pl.ds(k, ROOT, stride=TAPS), :]
        row, col = k // 2 * ROOT, k % 2 * ROOT
        m[row : row + ROOT, col : col + ROOT] = tw[2 + k].astype(BF)

    def relayout(i, carry):
        pltpu.make_async_copy(x_ref.at[i], xin.at[i], in_sem.at[i]).wait()
        for p in range(2):
            wide[p] = xin[i, p].astype(F32)
            for s in range(SPEC):
                frames[3 + s, i, p] = wide[p, pl.ds(s, ROOT, stride=SPEC), :].astype(BF)
        return carry

    lax.fori_loop(0, INP, relayout, 0)
    pl.semaphore_wait(barrier, 17)

    def halo(j):
        return pltpu.make_async_remote_copy(
            src_ref=frames.at[4 + j], dst_ref=frames.at[j],
            send_sem=halo_s.at[j], recv_sem=halo_r.at[j],
            device_id={"tm": (tm + 1) % 4}, device_id_type=MESH,
        )

    @pl.when(tm < 3)
    def _():
        for j in (2, 1, 0):
            halo(j).start()

    def spectrum(s):
        def pair(step, carry):
            sides = []
            for j in range(2):
                i = step * 2 + j
                parts = []
                for p in range(2):
                    total = taps[0] * frames[s, i, p].astype(F32)
                    for k in range(1, TAPS):
                        total = total + taps[k] * frames[s + k, i, p].astype(F32)
                    parts.append(total.astype(BF))
                sides.append(jnp.concatenate(parts, axis=0))
            both = jnp.concatenate(sides, axis=1)
            first = jnp.dot(m[...], both, preferred_element_type=F32)
            rows = []
            for j in range(2):
                real = first[:ROOT, j * ROOT : (j + 1) * ROOT]
                imag = first[ROOT:, j * ROOT : (j + 1) * ROOT]
                cosine, sine = tw[0], tw[1]
                rows.append(
                    jnp.concatenate(
                        [(real * cosine + imag * sine).astype(BF), (imag * cosine - real * sine).astype(BF)],
                        axis=1,
                    )
                )
            second = lax.dot_general(
                m[...], jnp.concatenate(rows, axis=0), NT, preferred_element_type=F32
            )
            for j in range(2):
                turned[pl.ds(step * 2 + j, 2 * ROOT, stride=INP), :] = second[:, j * ROOT : (j + 1) * ROOT]
            return carry

        lax.fori_loop(0, INP // 2, pair, 0)

        def pack(g, carry):
            for p in range(2):
                for d in range(2):
                    row = pl.multiple_of((p * ROOT + 2 * g + d) * INP, INP)
                    lane = (p * 2 + d) * ROOT
                    place = (g % 8, g // 8) if s in Z_FIRST else (g // 8, g % 8)
                    snd[s, place[0], place[1], :, lane : lane + ROOT] = turned[pl.ds(row, INP), :].astype(BF)
            return carry

        lax.fori_loop(0, 64, pack, 0)

    def remote(src, dst, send_sem, recv_sem, to_xy, to_z):
        return pltpu.make_async_remote_copy(
            src_ref=src, dst_ref=dst, send_sem=send_sem, recv_sem=recv_sem,
            device_id={"chan": chan_of(to_xy, to_z)}, device_id_type=MESH,
        )

    def z_copy(s, k):
        to, slot = (z + k) % 8, (11 - k) % 8
        if s in Z_FIRST and k != 4:
            src, dst = snd.at[s, to], mid.at[s, slot]
        elif k != 4:
            src, dst = mid.at[s, :, to], rcv.at[s, :, slot]
        elif s in Z_FIRST:
            src, dst = mid.at[s, LATE], late.at[s]
        else:
            src, dst = mid.at[s, :, to], late.at[s]
        return remote(src, dst, z_s.at[s, k], z_r.at[s, k], xy, to)

    def xy_copy(s, k):
        to = other_xy(k)
        if s in Z_FIRST:
            src, dst = mid.at[s, 0:LATE, to], rcv.at[s, xy, 0:LATE]
        else:
            src, dst = snd.at[s, to], mid.at[s, xy]
        return remote(src, dst, xy_s.at[s, k], xy_r.at[s, k], to, z)

    def xl_copy(s, k):
        to = other_xy(k)
        return remote(snd.at[s, (z + 4) % 8, to], mid.at[s, LATE, xy], xl_s.at[s, k], xl_r.at[s, k], to, z)

    def z_own(s):
        if s in Z_FIRST:
            return pltpu.make_async_copy(snd.at[s, z], mid.at[s, 3], loc_sem.at[s, 0])
        return pltpu.make_async_copy(mid.at[s, :, z], rcv.at[s, :, 3], loc_sem.at[s, 0])

    def xy_own(s):
        if s in Z_FIRST:
            return pltpu.make_async_copy(mid.at[s, 0:LATE, xy], rcv.at[s, xy, 0:LATE], loc_sem.at[s, 1])
        return pltpu.make_async_copy(snd.at[s, xy], mid.at[s, xy], loc_sem.at[s, 1])

    def xl_own(s):
        return pltpu.make_async_copy(snd.at[s, (z + 4) % 8, xy], mid.at[s, LATE, xy], loc_sem.at[s, 2])

    early = (3, 5, 2, 6, 1, 7)

    def send_z(s):
        for k in early:
            z_copy(s, k).start()
        z_own(s).start()

    def send_xy(s):
        for k in range(1, 8):
            xy_copy(s, k).start()
        xy_own(s).start()

    def send_xl(s):
        for k in range(1, 8):
            xl_copy(s, k).start()
        xl_own(s).start()

    def wait_z(s, some=early):
        for k in some:
            z_copy(s, k).wait_recv()

    def wait_xy(s):
        for k in range(1, 8):
            xy_copy(s, k).wait_recv()
        xy_own(s).wait()

    def wait_xl(s):
        for k in range(1, 8):
            xl_copy(s, k).wait_recv()
        xl_own(s).wait()

    def arrive(j):
        @pl.when(tm > 0)
        def _():
            halo(j).wait_recv()

    def rows_of(s, owner):
        return rcv[s, pl.ds(2 * owner, 2)].reshape(256, WIDE)

    def with_swapped(left):
        swapped = jnp.concatenate([left[:, 256:], -left[:, :256]], axis=1)
        return jnp.concatenate([left, swapped], axis=0)

    def product(s, owner, j):
        return lax.dot_general(with_swapped(rows_of(s, owner)), rows_of(s, j), NT, preferred_element_type=F32)

    def correlate(s, fresh):
        def step(n, carry):
            owner, j = n // 4, n % 4
            both = product(s, owner, j)
            if fresh:
                acc[owner, j] = both
            else:
                acc[owner, j] += both
            return carry

        lax.fori_loop(0, 16, step, 0)

    rcv[:, :, LATE] = jnp.zeros((SPEC, 8, INP, WIDE), BF)

    spectrum(3)
    send_z(3)
    arrive(2)
    spectrum(2)
    send_z(2)
    arrive(1)
    spectrum(1)
    wait_z(3)
    z_own(3).wait()
    send_xy(3)
    send_z(1)
    arrive(0)
    spectrum(0)
    send_xy(0)
    wait_z(2)
    z_own(2).wait()
    send_xy(2)
    wait_xy(0)
    send_z(0)
    for s in (3, 2, 1):
        send_xl(s)
    wait_xy(3)
    correlate(3, True)
    wait_z(1)
    z_own(1).wait()
    send_xy(1)
    wait_xy(2)
    correlate(2, False)
    for s in (3, 2, 1):
        wait_xl(s)
    wait_xy(1)
    correlate(1, False)
    wait_z(0, early[4:])
    for s in (3, 2, 1, 0):
        z_copy(s, 4).start()
    wait_z(0, early[:4])
    z_own(0).wait()

    factor = 1.0 / 4096.0

    def sib_copy(h, j):
        return pltpu.make_async_remote_copy(
            src_ref=sib_snd.at[h, j], dst_ref=sib_rcv.at[h, j], send_sem=sib_s.at[h, j], recv_sem=sib_r.at[h, j],
            device_id={"tm": sibling}, device_id_type=MESH,
        )

    def x_copy(j):
        return pltpu.make_async_remote_copy(
            src_ref=x_snd.at[j, :, 0:112], dst_ref=x_rcv.at[j, :, 0:112], send_sem=x_s.at[j], recv_sem=x_r.at[j],
            device_id={"tm": partner}, device_id_type=MESH,
        )

    def block(owner, j):
        return (acc[owner, j] + product(0, owner, j)) * factor

    def far(j, carry):
        sib_snd[0, j] = block((1 - x_hi) * 2 + 1 - core, j).astype(BF)
        sib_copy(0, j).start()
        both = block((1 - x_hi) * 2 + core, j)
        sib_copy(0, j).wait_recv()
        x_snd[j] = (both + sib_rcv[0, j].astype(F32)).astype(BF).reshape(4, 128, 256)
        x_copy(j).start()
        return carry

    lax.fori_loop(0, 4, far, 0)

    def near(j, carry):
        sib_snd[1, j] = block(x_hi * 2 + 1 - core, j).astype(BF)
        sib_copy(1, j).start()
        both = block(x_hi * 2 + core, j)
        sib_copy(1, j).wait_recv()
        mine[j] = both + sib_rcv[1, j].astype(F32)
        return carry

    lax.fori_loop(0, 4, near, 0)

    def late_part(s, fresh):
        z_copy(s, 4).wait_recv()
        rcv[s, :, LATE] = late[s]
        tail = late[s].reshape(128, WIDE)
        tail_both = with_swapped(tail)

        def step(o, carry):
            right = rows_of(s, o)
            column = lax.dot_general(with_swapped(right), tail, NT, preferred_element_type=F32)
            row = lax.dot_general(tail_both, right, NT, preferred_element_type=F32)
            if fresh:
                d1[o] = column
                d2[o] = row
            else:
                d1[o] += column
                d2[o] += row
            return carry

        lax.fori_loop(0, 4, step, 0)

    late_part(3, True)
    late_part(2, False)
    late_part(1, False)
    late_part(0, False)

    def d_rows(owner):
        re = d2[:, pl.ds(pl.multiple_of(owner * 32, 32), 32), :]
        im = d2[:, pl.ds(pl.multiple_of(owner * 32 + 128, 32), 32), :]
        return re * factor, im * factor

    def ds_copies(h):
        return [
            pltpu.make_async_remote_copy(
                src_ref=d1_snd.at[h], dst_ref=d1_rcv.at[h], send_sem=ds_s.at[h, 0], recv_sem=ds_r.at[h, 0],
                device_id={"tm": sibling}, device_id_type=MESH,
            ),
            pltpu.make_async_remote_copy(
                src_ref=d2_snd.at[h], dst_ref=d2_rcv.at[h], send_sem=ds_s.at[h, 1], recv_sem=ds_r.at[h, 1],
                device_id={"tm": sibling}, device_id_type=MESH,
            ),
        ]

    dx_copies = [
        pltpu.make_async_remote_copy(
            src_ref=d1_xs, dst_ref=d1_xr, send_sem=dx_s.at[0], recv_sem=dx_r.at[0],
            device_id={"tm": partner}, device_id_type=MESH,
        ),
        pltpu.make_async_remote_copy(
            src_ref=d2_xs, dst_ref=d2_xr, send_sem=dx_s.at[1], recv_sem=dx_r.at[1],
            device_id={"tm": partner}, device_id_type=MESH,
        ),
    ]

    for h, owner in ((0, (1 - x_hi) * 2 + 1 - core), (1, x_hi * 2 + 1 - core)):
        d1_snd[h] = (d1[owner] * factor).astype(BF)
        re, im = d_rows(owner)
        d2_snd[h, 0] = re.astype(BF)
        d2_snd[h, 1] = im.astype(BF)
        for copy in ds_copies(h):
            copy.start()
    owner = (1 - x_hi) * 2 + core
    for copy in ds_copies(0):
        copy.wait_recv()
    d1_xs[...] = (d1[owner] * factor + d1_rcv[0].astype(F32)).astype(BF)
    re, im = d_rows(owner)
    d2_xs[0] = (re + d2_rcv[0, 0].astype(F32)).astype(BF)
    d2_xs[1] = (im + d2_rcv[0, 1].astype(F32)).astype(BF)
    for copy in dx_copies:
        copy.start()

    for j in range(4):
        x_copy(j).wait_recv()
    for copy in ds_copies(1):
        copy.wait_recv()
    for copy in dx_copies:
        copy.wait_recv()

    owner = x_hi * 2 + core
    turn = (z + 5) % 8
    lanes = lax.broadcasted_iota(jnp.int32, (256, ROOT), 1)
    columns = [
        d1[owner, pl.ds(part * 256, 256)] * factor
        + d1_rcv[1, pl.ds(part * 256, 256)].astype(F32)
        + d1_xr[pl.ds(part * 256, 256)].astype(F32)
        for part in range(2)
    ]
    own_rows = d_rows(owner)
    for part in range(2):
        rows = own_rows[part] + d2_rcv[1, part].astype(F32) + d2_xr[part].astype(F32)
        for c in range(8):
            j, half = c // 2, (c % 2) * ROOT
            tile = mine[j, part * 256 : part * 256 + 256, half : half + ROOT] + x_rcv[
                j, part * 2 : part * 2 + 2, :, half : half + ROOT
            ].reshape(256, ROOT).astype(F32)
            moved = columns[part] if c == 7 else pltpu.roll(columns[part], 112 - 16 * c, 1)
            tile = jnp.where(lanes >= 112, moved, tile)
            pieces = []
            for v in range(2):
                pieces.append(tile[v * 128 : v * 128 + 112])
                pieces.append(rows[j, v * 16 : v * 16 + 16, half : half + ROOT])
            tile = pltpu.roll(jnp.concatenate(pieces, axis=0), turn * 16, 1)
            for v in range(2):
                for t in range(8):
                    to = pl.multiple_of(v * 128 + ((turn + t) % 8) * 16, 16)
                    at = part * 1024 + c * ROOT
                    out_ref[pl.ds(to, 16), at : at + ROOT] = tile[v * 128 + t * 16 : v * 128 + t * 16 + 16]

    for s in range(SPEC):
        for k in range(1, 8):
            z_copy(s, k).wait_send()
            xy_copy(s, k).wait_send()
    for s in Z_FIRST:
        for k in range(1, 8):
            xl_copy(s, k).wait_send()
    for j in range(4):
        sib_copy(0, j).wait_send()
        sib_copy(1, j).wait_send()
        x_copy(j).wait_send()
    for h in range(2):
        for copy in ds_copies(h):
            copy.wait_send()
    for copy in dx_copies:
        copy.wait_send()

    @pl.when(tm < 3)
    def _():
        for j in range(3):
            halo(j).wait_send()


def body(samples, filter_taps):
    x = samples.reshape(INP, 2, SPEC, ROOT, ROOT).transpose(0, 1, 3, 2, 4).reshape(INP, 2, SPEC * ROOT, ROOT)
    t = filter_taps.reshape(TAPS, ROOT, ROOT).transpose(1, 0, 2).reshape(TAPS * ROOT, ROOT)
    vmem = pl.BlockSpec(memory_space=pltpu.VMEM)
    hbm = pl.BlockSpec(memory_space=pl.ANY)
    dma = pltpu.SemaphoreType.DMA
    out = pl.pallas_call(
        kernel,
        out_shape=jax.ShapeDtypeStruct((256, 2048), F32),
        in_specs=[hbm, hbm, hbm],
        out_specs=vmem,
        scratch_shapes=[
            pltpu.VMEM((INP, 2, SPEC * ROOT, ROOT), BF),
            pltpu.VMEM((TAPS * ROOT, ROOT), F32),
            pltpu.VMEM((TAPS, ROOT, ROOT), F32),
            pltpu.VMEM((2 * ROOT, 2 * ROOT), BF),
            pltpu.VMEM((6, ROOT, ROOT), F32),
            pltpu.VMEM((2, SPEC * ROOT, ROOT), F32),
            pltpu.VMEM((7, INP, 2, ROOT, ROOT), BF),
            pltpu.VMEM((2 * ROOT * INP, ROOT), F32),
            pltpu.VMEM((SPEC, 8, 8, INP, WIDE), BF),
            pltpu.VMEM((SPEC, 8, 8, INP, WIDE), BF),
            pltpu.VMEM((SPEC, 8, 8, INP, WIDE), BF),
            pltpu.VMEM((SPEC, 8, INP, WIDE), BF),
            pltpu.VMEM((4, 4, 512, 256), F32),
            pltpu.VMEM((4, 512, 256), F32),
            pltpu.VMEM((2, 4, 512, 256), BF),
            pltpu.VMEM((2, 4, 512, 256), BF),
            pltpu.VMEM((4, 4, 128, 256), BF),
            pltpu.VMEM((4, 4, 128, 256), BF),
            pltpu.VMEM((4, 512, 128), F32),
            pltpu.VMEM((4, 256, 256), F32),
            pltpu.VMEM((2, 512, 128), BF),
            pltpu.VMEM((2, 512, 128), BF),
            pltpu.VMEM((2, 2, 4, 32, 256), BF),
            pltpu.VMEM((2, 2, 4, 32, 256), BF),
            pltpu.VMEM((512, 128), BF),
            pltpu.VMEM((512, 128), BF),
            pltpu.VMEM((2, 4, 32, 256), BF),
            pltpu.VMEM((2, 4, 32, 256), BF),
            dma((INP,)), dma((3,)), dma((3,)), dma((3,)),
            dma((SPEC, 8)), dma((SPEC, 8)),
            dma((SPEC, 8)), dma((SPEC, 8)),
            dma((SPEC, 8)), dma((SPEC, 8)),
            dma((SPEC, 3)),
            dma((2, 4)), dma((2, 4)), dma((4,)), dma((4,)),
            dma((2, 2)), dma((2, 2)), dma((2,)), dma((2,)),
        ],
        compiler_params=pltpu.CompilerParams(
            collective_id=0, has_side_effects=True, vmem_limit_bytes=48 * 2**20
        ),
    )(x, t, jnp.asarray(tables()))
    return out[None]


def solution(mesh):
    placed = (P("chan", None, "tm", None), P())
    return jax.shard_map(
        body, mesh=mesh, in_specs=placed, out_specs=P("chan", "tm", None), check_vma=False
    )
```

time: 161 us -> 131 us (0.81)
  Pallas kernels: 155 us -> 128 us
  local copies, waits for them, and re-layouts: 6.02 us -> 3.27 us
    pallas_call x2 -> x1, Pallas kernels: 155 us -> 128 us  [body(): pl.pallas_call(kernel, out_shape=jax.ShapeDtypeStruct((256, 2048), F32),...]
    unnamed x8 -> x5, local copies, waits for them, and re-layouts: 6.02 us -> 3.27 us
where the time goes in v2:
time: 131 us
  Pallas kernels  128 us (98%)
  local copies, waits for them, and re-layouts  3.27 us (2%)
    pallas_call x1, Pallas kernels, body(): pl.pallas_call(kernel, out_shape=jax.ShapeDtypeStruct((256, 2048), F32),...  128 us
    unnamed x5, local copies, waits for them, and re-layouts  3.27 us

profile of v2, /device:TPU:1, one launch (start us, length us, event | category | flops | bytes accessed | tf_op | source)
XLA Modules:
  0.0 130.8 jit_solution(11092866300504415416)
XLA Ops:
  0.0 0.0 copy-start
  0.0 1.0 copy-done
  1.0 0.0 copy-start.1
  1.0 0.9 copy-done.1
  1.9 127.5 %shard_map.37 = f32[256,2048]{1,0:T(8,128)S(1)} custom-call(bf16[16,2,512,128]{3,2,1,0:T(8,128)(2,1)} %bitcast.13, f32[512,128]{1,0:T(8,128)S(1)} %bitcast.12, f32[6,128,128]{2,1,0:T(8,128)S(1)} %copy-done), custom_call_target="tpu_custom_call" | custom-call | tf_op jit(solution)/shard_map/pallas_call | solution.py:475
  129.5 1.3 %copy.7 = f32[1,256,2048]{2,1,0:T(8,128)} copy(f32[1,256,2048]{2,1,0:T(8,128)S(1)} %bitcast.11) | data formatting | bytes 4194304
Async XLA Ops:
  0.0 1.0 copy-start
  1.0 0.9 copy-start.1

commit v3 on v2

v3 whole, which is shorter than its diff:
```python
import math

import jax
import jax.numpy as jnp
import numpy as np
from jax import lax
from jax.experimental import pallas as pl
from jax.experimental.pallas import tpu as pltpu
from jax.sharding import PartitionSpec as P

ROOT = 128
TAPS = 4
SPEC = 4
INP = 16
GROUP = 4
HOP = 4
WIDE = 4 * ROOT
LATE = 7
ROWS = LATE * 2 * INP
Z_FIRST = (3, 2, 1)
MESH = pl.DeviceIdType.MESH
BF = jnp.bfloat16
F32 = jnp.float32
NT = (((1,), (1,)), ((), ()))


def dft_table():
    indices = np.arange(ROOT)
    angles = (indices[:, None] * indices[None, :] % ROOT) * (2.0 * math.pi / ROOT)
    cosine, sine = np.cos(angles), np.sin(angles)
    upper = np.concatenate([cosine, sine], axis=1)
    lower = np.concatenate([-sine, cosine], axis=1)
    return np.concatenate([upper, lower], axis=0)


def twiddle_table():
    indices = np.arange(ROOT)
    angles = (indices[:, None] * indices[None, :]) * (2.0 * math.pi / (ROOT * ROOT))
    return np.stack([np.cos(angles), np.sin(angles)]) / ROOT


def tables():
    quarters = dft_table().reshape(2, ROOT, 2, ROOT).transpose(0, 2, 1, 3).reshape(4, ROOT, ROOT)
    return np.concatenate([twiddle_table(), quarters]).astype(np.float32).reshape(6 * ROOT, ROOT)


def kernel(
    x_ref, tab_ref, out_ref,
    xin, tin, taps, m, wide, frames, hop, turned, snd, mid, rcv,
    acc, acc3, left, mine, sib_snd, sib3_snd, sib_rcv, sib3_rcv, x_snd, x3_snd, x_rcv, x3_rcv,
    d1, d2, d1_snd, d1_rcv, d2_snd, d2_rcv, d1_xs, d1_xr, d2_xs, d2_xr,
    in_sem, const_sem, halo_s, halo_r, hop_s, hop_r, newest_s, newest_r, z_s, z_r, xy_s, xy_r, xl_s, xl_r, loc_sem,
    sib_s, sib_r, x_s, x_r, ds_s, ds_r, dx_s, dx_r,
):
    chan, tm = lax.axis_index("chan"), lax.axis_index("tm")
    x_lo, y, z = chan // 32, (chan // 8) % 4, chan % 8
    x_hi, core = tm // 2, tm % 2
    xy = x_lo * 4 + y
    sibling = x_hi * 2 + 1 - core
    partner = (1 - x_hi) * 2 + core

    def chan_of(xy_, z_):
        return xy_ * 8 + z_

    def other_xy(k):
        return ((x_lo + k // 4) % 2) * 4 + (y + k % 4) % 4

    constants = pltpu.make_async_copy(tab_ref, tin, const_sem.at[0])
    constants.start()
    for i in range(INP):
        pltpu.make_async_copy(x_ref.at[i], xin.at[i], in_sem.at[i]).start()

    barrier = pltpu.get_barrier_semaphore()
    for k in range(1, 8):
        pl.semaphore_signal(barrier, inc=1, device_id={"chan": chan_of(xy, (z + k) % 8)}, device_id_type=MESH)
        pl.semaphore_signal(barrier, inc=1, device_id={"chan": chan_of(other_xy(k), z)}, device_id_type=MESH)
    for k in range(1, 4):
        pl.semaphore_signal(barrier, inc=1, device_id={"tm": (tm + k) % 4}, device_id_type=MESH)
    pl.semaphore_signal(
        barrier, inc=1, device_id={"chan": chan_of(other_xy(4), z), "tm": (tm + 3) % 4}, device_id_type=MESH
    )

    @pl.when(tm == 0)
    def _():
        frames[0:3] = jnp.zeros((3, INP, 2, ROOT, ROOT), BF)

    constants.wait()
    for k in range(4):
        taps[k] = tin[pl.ds(k, ROOT, stride=TAPS), :]
        row, col = k // 2 * ROOT, k % 2 * ROOT
        m[row : row + ROOT, col : col + ROOT] = tin[(6 + k) * ROOT : (7 + k) * ROOT].astype(BF)

    pl.semaphore_wait(barrier, 18)

    def halo(j, rest):
        inputs = slice(INP - HOP, INP) if rest else slice(0, INP - HOP)
        return pltpu.make_async_remote_copy(
            src_ref=frames.at[4 + j, inputs], dst_ref=frames.at[j, inputs],
            send_sem=halo_s.at[rest, j], recv_sem=halo_r.at[rest, j],
            device_id={"tm": (tm + 1) % 4}, device_id_type=MESH,
        )

    def hop_out(j):
        return pltpu.make_async_remote_copy(
            src_ref=frames.at[4 + j, INP - HOP : INP], dst_ref=hop.at[j],
            send_sem=halo_s.at[1, j], recv_sem=hop_r.at[j],
            device_id={"chan": chan_of(other_xy(4), z), "tm": (tm + 1) % 4}, device_id_type=MESH,
        )

    def hop_on(j):
        return pltpu.make_async_remote_copy(
            src_ref=hop.at[j], dst_ref=frames.at[j, INP - HOP : INP],
            send_sem=hop_s.at[j], recv_sem=halo_r.at[1, j],
            device_id={"chan": chan_of(other_xy(4), z)}, device_id_type=MESH,
        )

    def newest(step):
        inputs = pl.ds(step * GROUP, GROUP)
        return pltpu.make_async_remote_copy(
            src_ref=frames.at[6, inputs], dst_ref=frames.at[2, inputs],
            send_sem=newest_s.at[step], recv_sem=newest_r.at[step],
            device_id={"tm": (tm + 1) % 4}, device_id_type=MESH,
        )

    def transform(start, sides):
        for a in range(0, GROUP, 2):
            first = jnp.dot(m[...], jnp.concatenate(sides[a : a + 2], axis=1), preferred_element_type=F32)
            rows = []
            for j in range(2):
                real = first[:ROOT, j * ROOT : (j + 1) * ROOT]
                imag = first[ROOT:, j * ROOT : (j + 1) * ROOT]
                cosine, sine = tin[4 * ROOT : 5 * ROOT], tin[5 * ROOT : 6 * ROOT]
                rows.append(
                    jnp.concatenate(
                        [(real * cosine + imag * sine).astype(BF), (imag * cosine - real * sine).astype(BF)],
                        axis=1,
                    )
                )
            second = lax.dot_general(
                m[...], jnp.concatenate(rows, axis=0), NT, preferred_element_type=F32
            )
            for j in range(2):
                turned[pl.ds(start + a + j, 2 * ROOT, stride=INP), :] = second[:, j * ROOT : (j + 1) * ROOT]

    def pack(s):
        def step(g, carry):
            for v in range(8):
                for p in range(2):
                    for d in range(2):
                        row = pl.multiple_of((p * ROOT + 2 * (g * 8 + v) + d) * INP, INP)
                        lane = (p * 2 + d) * ROOT
                        place = (v, g) if s in Z_FIRST else (g, v)
                        snd[s, place[0], place[1], :, lane : lane + ROOT] = turned[pl.ds(row, INP), :].astype(BF)
            return carry

        lax.fori_loop(0, 8, step, 0)

    def first_spectrum():
        def group(step, carry):
            sides = []
            for j in range(GROUP):
                i = step * GROUP + j
                pltpu.make_async_copy(x_ref.at[i], xin.at[i], in_sem.at[i]).wait()
                parts = []
                for p in range(2):
                    wide[2 * j + p] = xin[i, p].astype(F32)
                    total = None
                    for k in range(TAPS):
                        frame = wide[2 * j + p, pl.ds(k, ROOT, stride=SPEC), :]
                        frames[3 + k, i, p] = frame.astype(BF)
                        total = taps[k] * frame if k == 0 else total + taps[k] * frame
                    parts.append(total.astype(BF))
                sides.append(jnp.concatenate(parts, axis=0))

            @pl.when(tm < 3)
            def _():
                newest(step).start()

            transform(step * GROUP, sides)
            return carry

        lax.fori_loop(0, INP // GROUP, group, 0)

        @pl.when(tm == 1)
        def _():
            hop_out(1).start()
            hop_out(0).start()

        @pl.when((tm == 0) | (tm == 2))
        def _():
            halo(1, 1).start()
            halo(0, 1).start()

        @pl.when(tm < 3)
        def _():
            halo(1, 0).start()
            halo(0, 0).start()

        pack(3)

    def spectrum(s):
        def group(step, carry):
            sides = []
            for j in range(GROUP):
                i = step * GROUP + j
                parts = []
                for p in range(2):
                    total = taps[0] * frames[s, i, p].astype(F32)
                    for k in range(1, TAPS):
                        total = total + taps[k] * frames[s + k, i, p].astype(F32)
                    parts.append(total.astype(BF))
                sides.append(jnp.concatenate(parts, axis=0))
            transform(step * GROUP, sides)
            return carry

        lax.fori_loop(0, INP // GROUP, group, 0)
        pack(s)

    def remote(src, dst, send_sem, recv_sem, to_xy, to_z):
        return pltpu.make_async_remote_copy(
            src_ref=src, dst_ref=dst, send_sem=send_sem, recv_sem=recv_sem,
            device_id={"chan": chan_of(to_xy, to_z)}, device_id_type=MESH,
        )

    def z_copy(s, k):
        to, slot = (z + k) % 8, (11 - k) % 8
        if s in Z_FIRST and k != 4:
            src, dst = snd.at[s, to], mid.at[s, slot]
        elif k != 4:
            src, dst = mid.at[s, :, to], rcv.at[s, slot]
        elif s in Z_FIRST:
            src, dst = mid.at[s, LATE], rcv.at[s, LATE]
        else:
            src, dst = mid.at[s, :, to], rcv.at[s, LATE]
        return remote(src, dst, z_s.at[s, k], z_r.at[s, k], xy, to)

    def xy_copy(s, k):
        to = other_xy(k)
        if s in Z_FIRST:
            src, dst = mid.at[s, 0:LATE, to], rcv.at[s, 0:LATE, xy]
        else:
            src, dst = snd.at[s, to], mid.at[s, xy]
        return remote(src, dst, xy_s.at[s, k], xy_r.at[s, k], to, z)

    def xl_copy(s, k):
        to = other_xy(k)
        return remote(snd.at[s, (z + 4) % 8, to], mid.at[s, LATE, xy], xl_s.at[s, k], xl_r.at[s, k], to, z)

    def z_own(s):
        if s in Z_FIRST:
            return pltpu.make_async_copy(snd.at[s, z], mid.at[s, 3], loc_sem.at[s, 0])
        return pltpu.make_async_copy(mid.at[s, :, z], rcv.at[s, 3], loc_sem.at[s, 0])

    def xy_own(s):
        if s in Z_FIRST:
            return pltpu.make_async_copy(mid.at[s, 0:LATE, xy], rcv.at[s, 0:LATE, xy], loc_sem.at[s, 1])
        return pltpu.make_async_copy(snd.at[s, xy], mid.at[s, xy], loc_sem.at[s, 1])

    def xl_own(s):
        return pltpu.make_async_copy(snd.at[s, (z + 4) % 8, xy], mid.at[s, LATE, xy], loc_sem.at[s, 2])

    early = (3, 5, 2, 6, 1, 7)

    def send_z(s):
        for k in early:
            z_copy(s, k).start()
        z_own(s).start()

    def send_xy(s):
        for k in range(1, 8):
            xy_copy(s, k).start()
        xy_own(s).start()

    def send_xl(s):
        for k in range(1, 8):
            xl_copy(s, k).start()
        xl_own(s).start()

    def wait_z(s, some=early):
        for k in some:
            z_copy(s, k).wait_recv()

    def wait_xy(s):
        for k in range(1, 8):
            xy_copy(s, k).wait_recv()
        xy_own(s).wait()

    def wait_xl(s):
        for k in range(1, 8):
            xl_copy(s, k).wait_recv()
        xl_own(s).wait()

    def pass_on():
        @pl.when(tm == 2)
        def _():
            for j in (1, 0):
                hop_out(j).wait_recv()
                hop_on(j).start()

    def arrive(j):
        @pl.when(tm > 0)
        def _():
            if j == 2:
                for step in range(INP // GROUP):
                    newest(step).wait_recv()
            else:
                halo(j, 0).wait_recv()
                halo(j, 1).wait_recv()

    def rows_of(s, owner):
        return rcv[s, 0:LATE, pl.ds(2 * owner, 2)].reshape(ROWS, WIDE)

    def columns_of(s, j):
        if j == 3:
            return rcv[s, 6].reshape(ROOT, WIDE)
        return rcv[s, 2 * j : 2 * j + 2].reshape(256, WIDE)

    def with_swapped(left):
        swapped = jnp.concatenate([left[:, 256:], -left[:, :256]], axis=1)
        return jnp.concatenate([left, swapped], axis=0)

    def times(left, right):
        return lax.dot_general(left, right, NT, preferred_element_type=F32)

    def piece(refs, j):
        return refs[1] if j == 3 else refs[0].at[j]

    def acc_of(owner, j):
        return acc3.at[owner] if j == 3 else acc.at[owner, j]

    def correlate(s, fresh):
        def step(owner, carry):
            left = with_swapped(rows_of(s, owner))
            for j in range(4):
                both = times(left, columns_of(s, j))
                if fresh:
                    acc_of(owner, j)[...] = both
                else:
                    acc_of(owner, j)[...] += both
            return carry

        lax.fori_loop(0, 4, step, 0)

    first_spectrum()
    send_z(3)
    arrive(2)
    mine[LATE] = jnp.zeros((512, ROOT), F32)
    spectrum(2)
    send_z(2)
    pass_on()
    arrive(1)
    spectrum(1)
    wait_z(3)
    z_own(3).wait()
    send_xy(3)
    send_z(1)
    arrive(0)
    spectrum(0)
    send_xy(0)
    wait_z(2)
    z_own(2).wait()
    send_xy(2)
    wait_xy(0)
    send_z(0)
    for s in (3, 2, 1):
        send_xl(s)
    wait_xy(3)
    correlate(3, True)
    wait_z(1)
    z_own(1).wait()
    send_xy(1)
    wait_xy(2)
    correlate(2, False)
    for s in (3, 2, 1):
        wait_xl(s)
    wait_xy(1)
    wait_z(0, early[4:])
    for s in (3, 2, 1, 0):
        z_copy(s, 4).start()
    wait_z(0, early[:4])
    z_own(0).wait()

    factor = 1.0 / 4096.0

    def part_of(refs, h, j):
        return refs[1].at[h] if j == 3 else refs[0].at[h, j]

    def sib_copy(h, j):
        return pltpu.make_async_remote_copy(
            src_ref=part_of((sib_snd, sib3_snd), h, j), dst_ref=part_of((sib_rcv, sib3_rcv), h, j),
            send_sem=sib_s.at[h, j], recv_sem=sib_r.at[h, j],
            device_id={"tm": sibling}, device_id_type=MESH,
        )

    def x_copy(j):
        return pltpu.make_async_remote_copy(
            src_ref=piece((x_snd, x3_snd), j), dst_ref=piece((x_rcv, x3_rcv), j),
            send_sem=x_s.at[j], recv_sem=x_r.at[j],
            device_id={"tm": partner}, device_id_type=MESH,
        )

    def block(owner, side, j):
        last = times(left[side, 0], columns_of(0, j)) + times(left[side, 1], columns_of(1, j))
        return (acc_of(owner, j)[...] + last) * factor

    def store_mine(j, both):
        for part in range(2):
            rows = both[part * ROWS : part * ROWS + ROWS]
            mine[2 * j, part * 256 : part * 256 + ROWS] = rows[:, :ROOT]
            if j < 3:
                mine[2 * j + 1, part * 256 : part * 256 + ROWS] = rows[:, ROOT:]

    for h, hi in ((0, 1 - x_hi), (1, x_hi)):
        given, kept = hi * 2 + 1 - core, hi * 2 + core
        for s in range(2):
            left[0, s] = with_swapped(rows_of(s, given))
            left[1, s] = with_swapped(rows_of(s, kept))

        def give(j):
            both = block(given, 0, j)
            part_of((sib_snd, sib3_snd), h, j)[...] = both.astype(BF)
            sib_copy(h, j).start()

        def keep(j):
            both = block(kept, 1, j)
            sib_copy(h, j).wait_recv()
            both = both + part_of((sib_rcv, sib3_rcv), h, j)[...].astype(F32)
            if h == 0:
                piece((x_snd, x3_snd), j)[...] = both.astype(BF)
                x_copy(j).start()
            else:
                store_mine(j, both)

        give(0)
        give(1)
        keep(0)
        give(2)
        keep(1)
        give(3)
        keep(2)
        keep(3)

    def late_part(s, fresh):
        z_copy(s, 4).wait_recv()
        tail = rcv[s, LATE].reshape(ROOT, WIDE)
        tail_both = with_swapped(tail)

        def column(o, carry):
            both = times(with_swapped(rows_of(s, o)), tail)
            if fresh:
                d1[o] = both
            else:
                d1[o] += both
            return carry

        lax.fori_loop(0, 4, column, 0)

        def row(j, carry):
            both = times(tail_both, rcv[s, pl.ds(2 * j, 2)].reshape(256, WIDE))
            if fresh:
                d2[j] = both
            else:
                d2[j] += both
            return carry

        lax.fori_loop(0, 4, row, 0)

    late_part(3, True)
    late_part(2, False)
    late_part(1, False)
    late_part(0, False)

    def d_rows(owner):
        re = d2[:, pl.ds(pl.multiple_of(owner * 32, 32), 32), :]
        im = d2[:, pl.ds(pl.multiple_of(owner * 32 + 128, 32), 32), :]
        return re * factor, im * factor

    def ds_copies(h):
        return [
            pltpu.make_async_remote_copy(
                src_ref=d1_snd.at[h], dst_ref=d1_rcv.at[h], send_sem=ds_s.at[h, 0], recv_sem=ds_r.at[h, 0],
                device_id={"tm": sibling}, device_id_type=MESH,
            ),
            pltpu.make_async_remote_copy(
                src_ref=d2_snd.at[h], dst_ref=d2_rcv.at[h], send_sem=ds_s.at[h, 1], recv_sem=ds_r.at[h, 1],
                device_id={"tm": sibling}, device_id_type=MESH,
            ),
        ]

    dx_copies = [
        pltpu.make_async_remote_copy(
            src_ref=d1_xs, dst_ref=d1_xr, send_sem=dx_s.at[0], recv_sem=dx_r.at[0],
            device_id={"tm": partner}, device_id_type=MESH,
        ),
        pltpu.make_async_remote_copy(
            src_ref=d2_xs, dst_ref=d2_xr, send_sem=dx_s.at[1], recv_sem=dx_r.at[1],
            device_id={"tm": partner}, device_id_type=MESH,
        ),
    ]

    for h, owner in ((0, (1 - x_hi) * 2 + 1 - core), (1, x_hi * 2 + 1 - core)):
        d1_snd[h] = (d1[owner] * factor).astype(BF)
        re, im = d_rows(owner)
        d2_snd[h, 0] = re.astype(BF)
        d2_snd[h, 1] = im.astype(BF)
        for copy in ds_copies(h):
            copy.start()
    owner = (1 - x_hi) * 2 + core
    for copy in ds_copies(0):
        copy.wait_recv()
    d1_xs[...] = (d1[owner] * factor + d1_rcv[0].astype(F32)).astype(BF)
    re, im = d_rows(owner)
    d2_xs[0] = (re + d2_rcv[0, 0].astype(F32)).astype(BF)
    d2_xs[1] = (im + d2_rcv[0, 1].astype(F32)).astype(BF)
    for copy in dx_copies:
        copy.start()

    turn = (z + 5) % 8
    block_of = lax.broadcasted_iota(jnp.int32, (32, ROOT), 1) // INP

    def transposed(tiles):
        for bit in (1, 2, 4):
            low = block_of // bit % 2 == 0
            swapped = list(tiles)
            for a in range(8):
                if a & bit == 0:
                    one, two = tiles[a], tiles[a | bit]
                    swapped[a] = jnp.where(low, one, pltpu.roll(two, bit * INP, 1))
                    swapped[a | bit] = jnp.where(low, pltpu.roll(one, ROOT - bit * INP, 1), two)
            tiles = swapped
        return tiles

    for j in range(4):
        x_copy(j).wait_recv()
        for part in range(2):
            rows = piece((x_rcv, x3_rcv), j)[part * ROWS : part * ROWS + ROWS].astype(F32)
            mine[2 * j, part * 256 : part * 256 + ROWS] += rows[:, :ROOT]
            if j < 3:
                mine[2 * j + 1, part * 256 : part * 256 + ROWS] += rows[:, ROOT:]

    def place(part, t):
        at = pl.ds(pl.multiple_of(part * 256 + t * 32, 32), 32)
        tiles = transposed([mine[(g + 8 - turn) % 8, at, :] for g in range(8)])
        for v in range(2):
            to = pl.ds(pl.multiple_of(v * ROOT + (turn + t) % 8 * INP, INP), INP)
            for c in range(8):
                out_ref[to, part * 1024 + c * ROOT : part * 1024 + c * ROOT + ROOT] = tiles[c][v * INP : v * INP + INP]

    def place_early(t, carry):
        for part in range(2):
            place(part, t)
        return carry

    lax.fori_loop(0, LATE, place_early, 0)

    owner = x_hi * 2 + core
    for copy in ds_copies(1):
        copy.wait_recv()
    own_rows = d_rows(owner)
    for copy in dx_copies:
        copy.wait_recv()

    last = (z + 4) % 8

    def place_columns(t, carry):
        for part in range(2):
            at = pl.ds(pl.multiple_of(part * ROWS + t * 32, 32), 32)
            both = d1[owner, at] * factor + d1_rcv[1, at].astype(F32) + d1_xr[at].astype(F32)
            both = pltpu.roll(both, last * INP, 1)
            for c in range(8):
                moved = both if c == 0 else pltpu.roll(both, ROOT - c * INP, 1)
                cols = slice(part * 1024 + c * ROOT, part * 1024 + c * ROOT + ROOT)
                for v in range(2):
                    to = pl.ds(pl.multiple_of(v * ROOT + (turn + t) % 8 * INP, INP), INP)
                    out_ref[to, cols] = jnp.where(
                        block_of[:INP] == last, moved[v * INP : v * INP + INP], out_ref[to, cols]
                    )
        return carry

    lax.fori_loop(0, LATE, place_columns, 0)

    for part in range(2):
        rows = own_rows[part] + d2_rcv[1, part].astype(F32) + d2_xr[part].astype(F32)
        for t in range(8):
            mine[t, part * 256 + ROWS : part * 256 + 256] = rows[t // 2, :, t % 2 * ROOT : t % 2 * ROOT + ROOT]
        place(part, LATE)

    for s in range(SPEC):
        for k in range(1, 8):
            z_copy(s, k).wait_send()
            xy_copy(s, k).wait_send()
    for s in Z_FIRST:
        for k in range(1, 8):
            xl_copy(s, k).wait_send()
    for j in range(4):
        sib_copy(0, j).wait_send()
        sib_copy(1, j).wait_send()
        x_copy(j).wait_send()
    for h in range(2):
        for copy in ds_copies(h):
            copy.wait_send()
    for copy in dx_copies:
        copy.wait_send()

    @pl.when(tm < 3)
    def _():
        for j in range(2):
            halo(j, 0).wait_send()
            halo(j, 1).wait_send()
        for step in range(INP // GROUP):
            newest(step).wait_send()

    @pl.when(tm == 2)
    def _():
        for j in range(2):
            hop_on(j).wait_send()


def body(samples, filter_taps):
    x = samples.reshape(INP, 2, SPEC, ROOT, ROOT).transpose(0, 1, 3, 2, 4).reshape(INP, 2, SPEC * ROOT, ROOT)
    t = filter_taps.reshape(TAPS, ROOT, ROOT).transpose(1, 0, 2).reshape(TAPS * ROOT, ROOT)
    vmem = pl.BlockSpec(memory_space=pltpu.VMEM)
    hbm = pl.BlockSpec(memory_space=pl.ANY)
    dma = pltpu.SemaphoreType.DMA
    out = pl.pallas_call(
        kernel,
        out_shape=jax.ShapeDtypeStruct((256, 2048), F32),
        in_specs=[hbm, hbm],
        out_specs=vmem,
        scratch_shapes=[
            pltpu.VMEM((INP, 2, SPEC * ROOT, ROOT), BF),
            pltpu.VMEM((10 * ROOT, ROOT), F32),
            pltpu.VMEM((TAPS, ROOT, ROOT), F32),
            pltpu.VMEM((2 * ROOT, 2 * ROOT), BF),
            pltpu.VMEM((2 * GROUP, SPEC * ROOT, ROOT), F32),
            pltpu.VMEM((7, INP, 2, ROOT, ROOT), BF),
            pltpu.VMEM((2, HOP, 2, ROOT, ROOT), BF),
            pltpu.VMEM((2 * ROOT * INP, ROOT), F32),
            pltpu.VMEM((SPEC, 8, 8, INP, WIDE), BF),
            pltpu.VMEM((SPEC, 8, 8, INP, WIDE), BF),
            pltpu.VMEM((SPEC, 8, 8, INP, WIDE), BF),
            pltpu.VMEM((4, 3, 2 * ROWS, 256), F32),
            pltpu.VMEM((4, 2 * ROWS, ROOT), F32),
            pltpu.VMEM((2, 2, 2 * ROWS, WIDE), BF),
            pltpu.VMEM((8, 512, ROOT), F32),
            pltpu.VMEM((2, 3, 2 * ROWS, 256), BF),
            pltpu.VMEM((2, 2 * ROWS, ROOT), BF),
            pltpu.VMEM((2, 3, 2 * ROWS, 256), BF),
            pltpu.VMEM((2, 2 * ROWS, ROOT), BF),
            pltpu.VMEM((3, 2 * ROWS, 256), BF),
            pltpu.VMEM((2 * ROWS, ROOT), BF),
            pltpu.VMEM((3, 2 * ROWS, 256), BF),
            pltpu.VMEM((2 * ROWS, ROOT), BF),
            pltpu.VMEM((4, 2 * ROWS, ROOT), F32),
            pltpu.VMEM((4, 256, 256), F32),
            pltpu.VMEM((2, 2 * ROWS, ROOT), BF),
            pltpu.VMEM((2, 2 * ROWS, ROOT), BF),
            pltpu.VMEM((2, 2, 4, 32, 256), BF),
            pltpu.VMEM((2, 2, 4, 32, 256), BF),
            pltpu.VMEM((2 * ROWS, ROOT), BF),
            pltpu.VMEM((2 * ROWS, ROOT), BF),
            pltpu.VMEM((2, 4, 32, 256), BF),
            pltpu.VMEM((2, 4, 32, 256), BF),
            dma((INP,)), dma((1,)), dma((2, 2)), dma((2, 2)), dma((2,)), dma((2,)),
            dma((INP // GROUP,)), dma((INP // GROUP,)),
            dma((SPEC, 8)), dma((SPEC, 8)),
            dma((SPEC, 8)), dma((SPEC, 8)),
            dma((SPEC, 8)), dma((SPEC, 8)),
            dma((SPEC, 3)),
            dma((2, 4)), dma((2, 4)), dma((4,)), dma((4,)),
            dma((2, 2)), dma((2, 2)), dma((2,)), dma((2,)),
        ],
        compiler_params=pltpu.CompilerParams(
            collective_id=0, has_side_effects=True, vmem_limit_bytes=50 * 2**20
        ),
    )(x, jnp.concatenate([t, jnp.asarray(tables())]))
    return out[None]


def solution(mesh):
    placed = (P("chan", None, "tm", None), P())
    return jax.shard_map(
        body, mesh=mesh, in_specs=placed, out_specs=P("chan", "tm", None), check_vma=False
    )
```

time: 131 us -> 128 us (0.977)
  Pallas kernels: 128 us -> 126 us
  local copies, waits for them, and re-layouts: 3.27 us -> 1.32 us
    unnamed x5 -> x1, local copies, waits for them, and re-layouts: 3.27 us -> 1.32 us
    pallas_call x1, Pallas kernels: 128 us -> 126 us  [body(): pl.pallas_call(kernel, out_shape=jax.ShapeDtypeStruct((256, 2048), F32),...]
where the time goes in v3:
time: 128 us
  Pallas kernels  126 us (98%)
  local copies, waits for them, and re-layouts  1.32 us (1%)
    pallas_call x1, Pallas kernels, body(): pl.pallas_call(kernel, out_shape=jax.ShapeDtypeStruct((256, 2048), F32),...  126 us

profile of v3, /device:TPU:1, one launch (start us, length us, event | category | flops | bytes accessed | tf_op | source)
XLA Modules:
  0.0 128.1 jit_solution(1681433116133244992)
XLA Ops:
  0.0 1.1 pad_maximum_fusion.tab_ref
  1.1 125.7 %shard_map.37 = f32[256,2048]{1,0:T(8,128)S(1)} custom-call(bf16[16,2,512,128]{3,2,1,0:T(8,128)(2,1)} %bitcast.12, f32[1280,128]{1,0:T(8,128)S(1)} %pad_maximum_fusion.tab_ref), custom_call_target="tpu_custom_call" | custom-call | tf_op jit(solution)/shard_map/pallas_call | solution.py:625
  126.8 1.3 %copy.7 = f32[1,256,2048]{2,1,0:T(8,128)} copy(f32[1,256,2048]{2,1,0:T(8,128)S(1)} %bitcast.11) | data formatting | bytes 4194304

commit v4 on v3

--- a/solution.py
+++ b/solution.py
@@ -13,7 +13,7 @@
 SPEC = 4
 INP = 16
 GROUP = 4
-HOP = 4
+HOP = 2
 WIDE = 4 * ROOT
 LATE = 7
 ROWS = LATE * 2 * INP
@@ -267,7 +267,7 @@
         z_own(s).start()
 
     def send_xy(s):
-        for k in range(1, 8):
+        for k in (5, 7, 6, 4, 2, 1, 3):
             xy_copy(s, k).start()
         xy_own(s).start()
 

time: 128 us -> 128 us (level)
  no operation moved by 1% of the time
where the time goes in v4:
time: 128 us; the launch traced here: 127 us
  Pallas kernels  125 us (98%)
  local copies, waits for them, and re-layouts  1.32 us (1%)
    pallas_call x1, Pallas kernels, body(): pl.pallas_call(kernel, out_shape=jax.ShapeDtypeStruct((256, 2048), F32),...  125 us

profile of v4, /device:TPU:1, one launch (start us, length us, event | category | flops | bytes accessed | tf_op | source)
XLA Modules:
  0.0 127.1 jit_solution(14295687873786010449)
XLA Ops:
  0.0 1.1 pad_maximum_fusion.tab_ref
  1.1 124.6 %shard_map.37 = f32[256,2048]{1,0:T(8,128)S(1)} custom-call(bf16[16,2,512,128]{3,2,1,0:T(8,128)(2,1)} %bitcast.12, f32[1280,128]{1,0:T(8,128)S(1)} %pad_maximum_fusion.tab_ref), custom_call_target="tpu_custom_call" | custom-call | tf_op jit(solution)/shard_map/pallas_call | solution.py:625
  125.8 1.3 %copy.7 = f32[1,256,2048]{2,1,0:T(8,128)} copy(f32[1,256,2048]{2,1,0:T(8,128)S(1)} %bitcast.11) | data formatting | bytes 4194304

commit v5 on v4

--- a/solution.py
+++ b/solution.py
@@ -498,22 +498,25 @@
         ),
     ]
 
-    for h, owner in ((0, (1 - x_hi) * 2 + 1 - core), (1, x_hi * 2 + 1 - core)):
+    def give_late(h, owner):
         d1_snd[h] = (d1[owner] * factor).astype(BF)
+        ds_copies(h)[0].start()
         re, im = d_rows(owner)
         d2_snd[h, 0] = re.astype(BF)
         d2_snd[h, 1] = im.astype(BF)
-        for copy in ds_copies(h):
-            copy.start()
+        ds_copies(h)[1].start()
+
+    give_late(0, (1 - x_hi) * 2 + 1 - core)
     owner = (1 - x_hi) * 2 + core
-    for copy in ds_copies(0):
-        copy.wait_recv()
+    ds_copies(0)[0].wait_recv()
     d1_xs[...] = (d1[owner] * factor + d1_rcv[0].astype(F32)).astype(BF)
+    dx_copies[0].start()
     re, im = d_rows(owner)
+    ds_copies(0)[1].wait_recv()
     d2_xs[0] = (re + d2_rcv[0, 0].astype(F32)).astype(BF)
     d2_xs[1] = (im + d2_rcv[0, 1].astype(F32)).astype(BF)
-    for copy in dx_copies:
-        copy.start()
+    dx_copies[1].start()
+    give_late(1, x_hi * 2 + 1 - core)
 
     turn = (z + 5) % 8
     block_of = lax.broadcasted_iota(jnp.int32, (32, ROOT), 1) // INP
@@ -557,8 +560,7 @@
     for copy in ds_copies(1):
         copy.wait_recv()
     own_rows = d_rows(owner)
-    for copy in dx_copies:
-        copy.wait_recv()
+    dx_copies[0].wait_recv()
 
     last = (z + 4) % 8
 
@@ -579,6 +581,7 @@
 
     lax.fori_loop(0, LATE, place_columns, 0)
 
+    dx_copies[1].wait_recv()
     for part in range(2):
         rows = own_rows[part] + d2_rcv[1, part].astype(F32) + d2_xr[part].astype(F32)
         for t in range(8):

time: 128 us -> 126 us (0.984)
  Pallas kernels: 125 us -> 123 us
    pallas_call x1, Pallas kernels: 125 us -> 123 us  [body(): pl.pallas_call(kernel, out_shape=jax.ShapeDtypeStruct((256, 2048), F32),...]
where the time goes in v5:
time: 126 us; the launch traced here: 125 us
  Pallas kernels  123 us (98%)
  local copies, waits for them, and re-layouts  1.32 us (1%)
    pallas_call x1, Pallas kernels, body(): pl.pallas_call(kernel, out_shape=jax.ShapeDtypeStruct((256, 2048), F32),...  123 us

profile of v5, /device:TPU:1, one launch (start us, length us, event | category | flops | bytes accessed | tf_op | source)
XLA Modules:
  0.0 125.1 jit_solution(9225506095809163416)
XLA Ops:
  0.0 1.1 pad_maximum_fusion.tab_ref
  1.1 122.7 %shard_map.37 = f32[256,2048]{1,0:T(8,128)S(1)} custom-call(bf16[16,2,512,128]{3,2,1,0:T(8,128)(2,1)} %bitcast.12, f32[1280,128]{1,0:T(8,128)S(1)} %pad_maximum_fusion.tab_ref), custom_call_target="tpu_custom_call" | custom-call | tf_op jit(solution)/shard_map/pallas_call | solution.py:628
  123.8 1.3 %copy.7 = f32[1,256,2048]{2,1,0:T(8,128)} copy(f32[1,256,2048]{2,1,0:T(8,128)S(1)} %bitcast.11) | data formatting | bytes 4194304

commit v6 on v5

--- a/solution.py
+++ b/solution.py
@@ -374,6 +374,8 @@
     for s in (3, 2, 1):
         wait_xl(s)
     wait_xy(1)
+    for side in range(2):
+        left[side, 1] = with_swapped(rows_of(1, (1 - x_hi) * 2 + (1 - core if side == 0 else core)))
     wait_z(0, early[4:])
     for s in (3, 2, 1, 0):
         z_copy(s, 4).start()
@@ -412,7 +414,7 @@
 
     for h, hi in ((0, 1 - x_hi), (1, x_hi)):
         given, kept = hi * 2 + 1 - core, hi * 2 + core
-        for s in range(2):
+        for s in range(1 if h == 0 else 2):
             left[0, s] = with_swapped(rows_of(s, given))
             left[1, s] = with_swapped(rows_of(s, kept))
 
@@ -431,14 +433,14 @@
             else:
                 store_mine(j, both)
 
+        give(3)
         give(0)
+        keep(3)
         give(1)
         keep(0)
         give(2)
         keep(1)
-        give(3)
         keep(2)
-        keep(3)
 
     def late_part(s, fresh):
         z_copy(s, 4).wait_recv()

time: 126 us -> 125 us (level)
  no operation moved by 1% of the time
where the time goes in v6:
time: 125 us
  Pallas kernels  123 us (98%)
  local copies, waits for them, and re-layouts  1.32 us (1%)
    pallas_call x1, Pallas kernels, body(): pl.pallas_call(kernel, out_shape=jax.ShapeDtypeStruct((256, 2048), F32),...  123 us

profile of v6, /device:TPU:1, one launch (start us, length us, event | category | flops | bytes accessed | tf_op | source)
XLA Modules:
  0.0 125.1 jit_solution(5804727614893277851)
XLA Ops:
  0.0 1.1 pad_maximum_fusion.tab_ref
  1.1 122.7 %shard_map.37 = f32[256,2048]{1,0:T(8,128)S(1)} custom-call(bf16[16,2,512,128]{3,2,1,0:T(8,128)(2,1)} %bitcast.12, f32[1280,128]{1,0:T(8,128)S(1)} %pad_maximum_fusion.tab_ref), custom_call_target="tpu_custom_call" | custom-call | tf_op jit(solution)/shard_map/pallas_call | solution.py:630
  123.8 1.3 %copy.7 = f32[1,256,2048]{2,1,0:T(8,128)} copy(f32[1,256,2048]{2,1,0:T(8,128)S(1)} %bitcast.11) | data formatting | bytes 4194304
